TPU v7x, 128 devices: a whole 4x4x4 slice. The times are simulated.
128 devices in a mesh: sx: 8 (over y, z_hi), sy: 16 (over x, z_lo, core).
Axes of the slice: x: 4, y: 4, z: 4 (z_hi: 2, z_lo: 2; z = z_hi * 2 + z_lo), core: 2. Of those that a mesh axis runs over, the one named last changes fastest.
Arguments:
- panel: bfloat16 [8, 16, 64, 4096], P('sx', 'sy'), may hold values from -6 to 6
- band: bfloat16 [8, 16, 8, 3, 512, 512], P('sx', 'sy'), may hold values from -0.0024414062 to 0.0024414062
- faces: bfloat16 [8, 16, 4, 1024, 1024], P('sx', 'sy'), may hold values from -0.005859375 to 0.005859375
- face_rows: int32 [8, 16, 4, 1024], P('sx', 'sy'), may hold values from 0 to 4095
- owner: int32 [128], replicated, may hold values from 0 to 127, each once
Outputs:
- coarse_rows: float32 [128, 5, 4096], P(('sx', 'sy'))
Inputs may be any that keep to these rules, and one draw needn't show every extreme that they name: owner names every index of 0 to 127 exactly once.
All inputs are finite; a program needn't handle non-finite values.
Results may differ from a plain program's by a relative error of at most 0.0029.
Values may be sent and summed in bfloat16 or wider, within the bound.
A program may use at most 128 MiB of HBM per device.

v0:
```python
import functools

import jax
import jax.numpy as jnp
from jax import lax
from jax.experimental import pallas as pl
from jax.experimental.pallas import tpu as pltpu
from jax.sharding import PartitionSpec as P

MESH = pl.DeviceIdType.MESH
F32, BF16 = jnp.float32, jnp.bfloat16
NX, NY = 8, 16
K, R, TB, NB, F = 64, 4096, 512, 8, 1024
TILES = 10
PARTS = [(0, 2), (6, 4), (2, 4)]
STEPS = [
    ('gather', 0),
    ('gather', 1),
    ('greet',),
    ('exchange', 0),
    ('exchange', 1),
    ('gather', 2),
    ('gather', 3),
    ('exchange', 2),
    ('exchange', 3),
    ('band', 0, 8),
    ('put_band',),
    ('first', 0),
    ('face_loads', 0, 1, 2, 3),
    ('face', 0),
    ('face', 1),
    ('face', 2),
    ('face', 3),
    ('owners',),
    ('arrived', 2),
    ('arrived', 3),
    ('block', 2),
    ('block', 3),
    ('first', 1),
    ('arrived', 0),
    ('arrived', 1),
    ('block', 0),
    ('block', 1),
    ('first', 2),
    ('second', 0),
    ('second', 1),
    ('second', 2),
    ('finish', 0),
    ('finish', 1),
    ('finish', 2),
    ('drain',),
]
BAND_ORDER = [(1, 4), (2, 4), (3, 8), (4, 8), (5, 8), (6, 8), (7, 8), (0, 8)]
FAR_PLANE = [(2, 2), (2, 1), (2, 3), (1, 2), (3, 2), (2, 0), (0, 2), (1, 1), (1, 3), (3, 1), (3, 3), (1, 0), (3, 0), (0, 1), (0, 3)]
FAR_STACK = [4, 5, 2, 3, 6, 7, 1]
PLANE, STACK = 16, 8


def dot_nn(a, b):
    return lax.dot_general(a, b, (((1,), (0,)), ((), ())), preferred_element_type=F32)


def dot_nt(a, b):
    return lax.dot_general(a, b, (((1,), (1,)), ((), ())), preferred_element_type=F32)


def split(value):
    high = value.astype(BF16)
    low = (value - high.astype(F32)).astype(BF16)
    return jnp.concatenate([high, low], axis=0)


def wait_bytes(ref, sem):
    pltpu.make_async_copy(ref, ref, sem).wait()


def kernel(
    panel, band, faces, rows, owner, out,
    pv, bv, fv, rv, ov, own, remote, pair, tmp, flat, *refs,
):
    x, y = lax.axis_index("sx"), lax.axis_index("sy")
    me = x * NY + y
    planes, picks, stacks, sems = refs[:3], refs[3:6], refs[6:9], refs[9:]
    load_sem, send_sem, recv_sem, hop_send, hop_recv = sems
    loads = []

    def load(source, target):
        copy = pltpu.make_async_copy(source, target, load_sem.at[len(loads)])
        copy.start()
        loads.append(copy)
        return copy

    load_panel, load_rows = load(panel, pv), load(rows, rv)
    load_band = [load(band.at[b], bv.at[b]) for b in range(NB)]
    load_faces = [load(faces.at[d], fv.at[d]) for d in range(4)]
    load_owner = load(owner, ov)

    p, q = (y >> 2) * 4 + (x >> 1), (x & 1) * 4 + (y & 3)

    def in_plane(a, b):
        return lax.rem((x >> 1) + b, 4) * 2 + (x & 1), lax.rem((y >> 2) + a, 4) * 4 + (y & 3)

    def in_stack(bits):
        return x ^ (bits >> 2), y ^ (bits & 3)

    barrier = pltpu.get_barrier_semaphore()

    def hello(device):
        pl.semaphore_signal(barrier, inc=1, device_id=device, device_id_type=MESH)

    has = [x > 0, x < NX - 1, y > 0, y < NY - 1]
    near = [(x - 1, y), (x + 1, y), (x, y - 1), (x, y + 1)]
    beyond = [
        jnp.logical_and(has[0], (x & 1) == 0), jnp.logical_and(has[1], (x & 1) == 1),
        jnp.logical_and(has[2], (y & 3) == 0), jnp.logical_and(has[3], (y & 3) == 3),
    ]
    for d in range(4):
        pl.when(beyond[d])(lambda d=d: hello(near[d]))
    for bits in FAR_STACK:
        hello(in_stack(bits))
    for a, b in FAR_PLANE:
        hello(in_plane(a, b))

    def greet():
        pl.semaphore_wait(barrier, PLANE + STACK - 2 + sum(far.astype(jnp.int32) for far in beyond))

    def exchange(d):
        @pl.when(has[d])
        def _():
            pltpu.make_async_remote_copy(
                src_ref=own.at[d], dst_ref=remote.at[d ^ 1], send_sem=send_sem.at[d], recv_sem=recv_sem.at[d ^ 1],
                device_id=near[d], device_id_type=MESH,
            ).start()

    def arrived(d):
        @pl.when(has[d])
        def _():
            wait_bytes(remote.at[d], recv_sem.at[d])

    def gather(d):
        stacked = jnp.concatenate([pv[:, h * 256:(h + 1) * 256] for h in range(16)], axis=0)
        for q in range(4):
            columns = slice(q * 256, (q + 1) * 256)
            index = rv[d:d + 1, columns]
            place, group = index & 255, index >> 8
            onehot = jnp.where(lax.broadcasted_iota(jnp.int32, (256, 256), 0) == place, 1.0, 0.0).astype(BF16)
            found = dot_nn(stacked, onehot)
            chosen = jnp.zeros((K, 256), F32)
            for h in range(16):
                chosen = jnp.where(group == h, found[h * K:(h + 1) * K], chosen)
            own[d, :, columns] = chosen.astype(BF16)

    def put(b, block):
        tmp[:, :K] = block
        even = tmp[pl.ds(0, 32, 2), :]
        odd = tmp[pl.ds(1, 32, 2), :]
        flat[2 * b:2 * b + 2] = jnp.concatenate([even[:, :K], odd[:, :K]], axis=1).astype(BF16).reshape(2, 16, 128)

    state = {"total": jnp.zeros((2 * K, K), F32), "band": 0}

    def band_part(start, stop):
        for c, need in BAND_ORDER[start:stop]:
            while state["band"] < need:
                load_band[state["band"]].wait()
                state["band"] += 1
            product = None
            for t in range(3):
                b = (c + 1 - t) % NB
                term = dot_nn(pv[:, b * TB:(b + 1) * TB], bv[b, t])
                product = term if product is None else product + term
            state["total"] = state["total"] + dot_nt(split(product), pv[:, c * TB:(c + 1) * TB])

    def put_band():
        put(0, state["total"][:K] + state["total"][K:])

    def face_loads(*ds):
        for d in ds:
            load_faces[d].wait()

    def face_product(d):
        for h in range(2):
            columns = slice(h * 512, (h + 1) * 512)
            pair[d, :, columns] = split(dot_nn(own[d], fv[d, :, columns]))

    def face_block(d):
        block = dot_nt(pair[d], remote[d])
        put(1 + d, jnp.where(has[d], block[:K] + block[K:], 0.0))

    def owners():
        load_owner.wait()
        source = lax.broadcasted_iota(jnp.int32, (STACK, NX * NY), 1)
        source_p, source_q = ((source >> 2) & 3) * 4 + (source >> 5), ((source >> 4) & 1) * 4 + (source & 3)
        other = lax.broadcasted_iota(jnp.int32, (STACK, NX * NY), 0)
        target = ((x >> 1) * 2 + (other >> 2)) * NY + (y >> 2) * 4 + (other & 3)
        found = jnp.logical_and(ov[...] == target, source_q == q)
        places = jnp.max(jnp.where(found, source_p, 0), axis=1, keepdims=True)
        state["places"] = [places[j, 0] for j in range(STACK)]
        state["mine"] = jnp.max(jnp.where(ov[...] == me, source_q[:1], 0), axis=1, keepdims=True)[0, 0]

    def first_hop(part):
        tiles, plane = pl.ds(*PARTS[part]), planes[part]
        for a, b in FAR_PLANE:
            pltpu.make_async_remote_copy(
                src_ref=flat.at[tiles], dst_ref=plane.at[p],
                send_sem=hop_send.at[part], recv_sem=hop_recv.at[part],
                device_id=in_plane(a, b), device_id_type=MESH,
            ).start()
        plane[p] = flat[tiles]

    def second_hop(part):
        plane, pick, stack = planes[part], picks[part], stacks[part]
        wait_bytes(plane.at[pl.ds(0, PLANE - 1)], hop_recv.at[part])
        for j in range(STACK):
            pick[j] = plane[state["places"][j]]
        for bits in FAR_STACK:
            pltpu.make_async_remote_copy(
                src_ref=pick.at[q ^ bits], dst_ref=stack.at[q],
                send_sem=hop_send.at[3 + part], recv_sem=hop_recv.at[3 + part],
                device_id=in_stack(bits), device_id_type=MESH,
            ).start()
        stack[q] = pick[q]

    def finish(part):
        tiles, stack = pl.ds(*PARTS[part]), stacks[part]
        wait_bytes(stack.at[pl.ds(0, STACK - 1)], hop_recv.at[3 + part])
        out[tiles] = stack[state["mine"]].astype(F32)

    def drain():
        for d in range(4):
            @pl.when(has[d])
            def _():
                wait_bytes(own.at[d], send_sem.at[d])
        for part in range(len(PARTS)):
            wait_bytes(planes[part].at[pl.ds(0, PLANE - 1)], hop_send.at[part])
            wait_bytes(stacks[part].at[pl.ds(0, STACK - 1)], hop_send.at[3 + part])

    actions = dict(
        greet=greet, exchange=exchange, arrived=arrived, gather=gather, band=band_part, put_band=put_band,
        face_loads=face_loads, face=face_product, block=face_block, owners=owners, first=first_hop, second=second_hop,
        finish=finish, drain=drain,
    )
    load_panel.wait()
    load_rows.wait()
    for name, *numbers in STEPS:
        actions[name](*numbers)


def shards(panel, band, faces, face_rows, owner):
    blocks = pl.pallas_call(
        kernel,
        out_shape=jax.ShapeDtypeStruct((TILES, 16, 128), F32),
        in_specs=[pl.BlockSpec(memory_space=pl.ANY)] * 5,
        out_specs=pl.BlockSpec(memory_space=pltpu.VMEM),
        scratch_shapes=[
            pltpu.VMEM((K, R), BF16),
            pltpu.VMEM((NB, 3, TB, TB), BF16),
            pltpu.VMEM((4, F, F), BF16),
            pltpu.VMEM((4, F), jnp.int32),
            pltpu.VMEM((1, NX * NY), jnp.int32),
            pltpu.VMEM((4, K, F), BF16),
            pltpu.VMEM((4, K, F), BF16),
            pltpu.VMEM((4, 2 * K, F), BF16),
            pltpu.VMEM((K, 128), F32),
            pltpu.VMEM((TILES, 16, 128), BF16),
            *[pltpu.VMEM((PLANE, count, 16, 128), BF16) for _, count in PARTS],
            *[pltpu.VMEM((STACK, count, 16, 128), BF16) for _, count in PARTS * 2],
            pltpu.SemaphoreType.DMA((3 + NB + 4,)),
            pltpu.SemaphoreType.DMA((4,)),
            pltpu.SemaphoreType.DMA((4,)),
            pltpu.SemaphoreType.DMA((6,)),
            pltpu.SemaphoreType.DMA((6,)),
        ],
        compiler_params=pltpu.CompilerParams(collective_id=0, has_side_effects=True, vmem_limit_bytes=58 << 20),
        name="coarse_blocks",
    )(panel[0, 0], band[0, 0], faces[0, 0], face_rows[0, 0], owner.reshape(1, NX * NY))
    return blocks.reshape(1, 5, 4096)


def solution(mesh):
    in_specs = (
        P("sx", "sy", None, None),
        P("sx", "sy", None, None, None, None),
        P("sx", "sy", None, None, None),
        P("sx", "sy", None, None),
        P(),
    )
    out_specs = P(("sx", "sy"), None, None)
    return jax.shard_map(shards, mesh=mesh, in_specs=in_specs, out_specs=out_specs, check_vma=False)
```

profile of v0, /device:TPU:1, one launch (start us, length us, event | category | flops | bytes accessed | tf_op | source)
XLA Modules:
  0.0 30.8 jit_solution(12917917567914712481)
XLA Ops:
  0.0 29.3 %coarse_blocks.1 = f32[10,16,128]{2,1,0:T(8,128)} custom-call(bf16[64,4096]{1,0:T(8,128)(2,1)} %bitcast.8, bf16[8,3,512,512]{3,2,1,0:T(8,128)(2,1)} %bitcast.6, bf16[4,1024,1024]{2,1,0:T(8,128)(2,1)} %bitcast.7, s32[4,1024]{1,0:T(4,128)} %bitcast.10, s32[1,128]{1,0:T(1,128)} %bitcast.11), custom_call_target="tpu_custom_call" | custom-call | tf_op jit(solution)/shard_map/coarse_blocks/pallas_call | solution.py:249
  29.3 1.5 %copy.9 = f32[1,5,4096]{2,0,1:T(1,128)} copy(f32[1,5,4096]{2,0,1:T(1,128)} %bitcast.9) | data formatting | bytes 163840
where the time goes:
time: 31 us; the launch traced here: 30.8 us
  Pallas kernels  29.3 us (95%)
  local copies, waits for them, and re-layouts  1.53 us (5%)
    pallas_call x1, Pallas kernels, shards(): pl.pallas_call(kernel, out_shape=jax.ShapeDtypeStruct((TILES, 16, 128), F...  29.3 us
    unnamed x1, local copies, waits for them, and re-layouts  1.53 us

commit v1 on v0

--- a/solution.py
+++ b/solution.py
@@ -9,18 +9,20 @@
 
 MESH = pl.DeviceIdType.MESH
 F32, BF16 = jnp.float32, jnp.bfloat16
+OUT = BF16
 NX, NY = 8, 16
 K, R, TB, NB, F = 64, 4096, 512, 8, 1024
 TILES = 10
-PARTS = [(0, 2), (6, 4), (2, 4)]
+ORDER = [0, 3, 4, 1, 2]
+PARTS = [(0, 2, True), (2, 4, True), (6, 4, False)]
 STEPS = [
     ('gather', 0),
     ('gather', 1),
+    ('gather_if', 0, 2, 3),
     ('greet',),
     ('exchange', 0),
     ('exchange', 1),
-    ('gather', 2),
-    ('gather', 3),
+    ('gather_if', 1, 2, 3),
     ('exchange', 2),
     ('exchange', 3),
     ('band', 0, 8),
@@ -33,22 +35,23 @@
     ('face', 3),
     ('owners',),
     ('arrived', 2),
+    ('block', 2),
     ('arrived', 3),
-    ('block', 2),
     ('block', 3),
     ('first', 1),
     ('arrived', 0),
+    ('block', 0),
     ('arrived', 1),
-    ('block', 0),
     ('block', 1),
     ('first', 2),
     ('second', 0),
+    ('second', 2),
     ('second', 1),
-    ('second', 2),
     ('finish', 0),
     ('finish', 1),
     ('finish', 2),
-    ('drain',),
+    ('drain_faces', 0, 1, 2, 3),
+    ('drain_parts', 0, 1, 2),
 ]
 BAND_ORDER = [(1, 4), (2, 4), (3, 8), (4, 8), (5, 8), (6, 8), (7, 8), (0, 8)]
 FAR_PLANE = [(2, 2), (2, 1), (2, 3), (1, 2), (3, 2), (2, 0), (0, 2), (1, 1), (1, 3), (3, 1), (3, 3), (1, 0), (3, 0), (0, 1), (0, 3)]
@@ -80,21 +83,9 @@
 ):
     x, y = lax.axis_index("sx"), lax.axis_index("sy")
     me = x * NY + y
-    planes, picks, stacks, sems = refs[:3], refs[3:6], refs[6:9], refs[9:]
+    n = len(PARTS)
+    planes, picks, stacks, sems = refs[:n], refs[n:2 * n], refs[2 * n:3 * n], refs[3 * n:]
     load_sem, send_sem, recv_sem, hop_send, hop_recv = sems
-    loads = []
-
-    def load(source, target):
-        copy = pltpu.make_async_copy(source, target, load_sem.at[len(loads)])
-        copy.start()
-        loads.append(copy)
-        return copy
-
-    load_panel, load_rows = load(panel, pv), load(rows, rv)
-    load_band = [load(band.at[b], bv.at[b]) for b in range(NB)]
-    load_faces = [load(faces.at[d], fv.at[d]) for d in range(4)]
-    load_owner = load(owner, ov)
-
     p, q = (y >> 2) * 4 + (x >> 1), (x & 1) * 4 + (y & 3)
 
     def in_plane(a, b):
@@ -118,6 +109,20 @@
         pl.when(beyond[d])(lambda d=d: hello(near[d]))
     for bits in FAR_STACK:
         hello(in_stack(bits))
+
+    loads = []
+
+    def load(source, target):
+        copy = pltpu.make_async_copy(source, target, load_sem.at[len(loads)])
+        copy.start()
+        loads.append(copy)
+        return copy
+
+    load_panel, load_rows = load(panel, pv), load(rows, rv)
+    load_band = [load(band.at[b], bv.at[b]) for b in range(NB)]
+    load_faces = [load(faces.at[d], fv.at[d]) for d in range(4)]
+    load_owner = load(owner, ov)
+
     for a, b in FAR_PLANE:
         hello(in_plane(a, b))
 
@@ -150,11 +155,20 @@
                 chosen = jnp.where(group == h, found[h * K:(h + 1) * K], chosen)
             own[d, :, columns] = chosen.astype(BF16)
 
+    late = (x & 1) == 1
+
+    def gather_if(is_late, *ds):
+        @pl.when(late if is_late else jnp.logical_not(late))
+        def _():
+            for d in ds:
+                gather(d)
+
     def put(b, block):
         tmp[:, :K] = block
         even = tmp[pl.ds(0, 32, 2), :]
         odd = tmp[pl.ds(1, 32, 2), :]
-        flat[2 * b:2 * b + 2] = jnp.concatenate([even[:, :K], odd[:, :K]], axis=1).astype(BF16).reshape(2, 16, 128)
+        slot = 2 * ORDER.index(b)
+        flat[slot:slot + 2] = jnp.concatenate([even[:, :K], odd[:, :K]], axis=1).astype(BF16).reshape(2, 16, 128)
 
     state = {"total": jnp.zeros((2 * K, K), F32), "band": 0}
 
@@ -188,56 +202,87 @@
 
     def owners():
         load_owner.wait()
-        source = lax.broadcasted_iota(jnp.int32, (STACK, NX * NY), 1)
+        source = lax.broadcasted_iota(jnp.int32, (PLANE, NX * NY), 1)
         source_p, source_q = ((source >> 2) & 3) * 4 + (source >> 5), ((source >> 4) & 1) * 4 + (source & 3)
-        other = lax.broadcasted_iota(jnp.int32, (STACK, NX * NY), 0)
-        target = ((x >> 1) * 2 + (other >> 2)) * NY + (y >> 2) * 4 + (other & 3)
-        found = jnp.logical_and(ov[...] == target, source_q == q)
-        places = jnp.max(jnp.where(found, source_p, 0), axis=1, keepdims=True)
-        state["places"] = [places[j, 0] for j in range(STACK)]
-        state["mine"] = jnp.max(jnp.where(ov[...] == me, source_q[:1], 0), axis=1, keepdims=True)[0, 0]
-
-    def first_hop(part):
-        tiles, plane = pl.ds(*PARTS[part]), planes[part]
+        other = lax.broadcasted_iota(jnp.int32, (PLANE, NX * NY), 0)
+
+        def latest(match, value):
+            return jnp.max(jnp.where(match, value, 0), axis=1, keepdims=True)
+
+        target = ((x >> 1) * 2 + ((other >> 2) & 1)) * NY + (y >> 2) * 4 + (other & 3)
+        places = latest(jnp.logical_and(ov[...] == target, source_q == q), source_p)
+        state["from_plane"] = [places[j, 0] for j in range(STACK)]
+        target = ((other & 3) * 2 + (x & 1)) * NY + (other >> 2) * 4 + (y & 3)
+        places = latest(jnp.logical_and(ov[...] == target, source_p == p), source_q)
+        state["from_stack"] = [places[j, 0] for j in range(PLANE)]
+        state["mine"] = [latest(ov[...] == me, value[:1])[0, 0] for value in (source_p, source_q)]
+
+    def to_plane(source, target, sems):
         for a, b in FAR_PLANE:
             pltpu.make_async_remote_copy(
-                src_ref=flat.at[tiles], dst_ref=plane.at[p],
-                send_sem=hop_send.at[part], recv_sem=hop_recv.at[part],
-                device_id=in_plane(a, b), device_id_type=MESH,
+                src_ref=source(lax.rem((y >> 2) + a, 4) * 4 + lax.rem((x >> 1) + b, 4)), dst_ref=target.at[p],
+                send_sem=hop_send.at[sems], recv_sem=hop_recv.at[sems], device_id=in_plane(a, b), device_id_type=MESH,
             ).start()
-        plane[p] = flat[tiles]
+
+    def to_stack(source, target, sems):
+        for bits in FAR_STACK:
+            pltpu.make_async_remote_copy(
+                src_ref=source(q ^ bits), dst_ref=target.at[q],
+                send_sem=hop_send.at[sems], recv_sem=hop_recv.at[sems], device_id=in_stack(bits), device_id_type=MESH,
+            ).start()
+
+    def first_hop(part):
+        first, count, plane_first = PARTS[part]
+        tiles = pl.ds(first, count)
+        if plane_first:
+            to_plane(lambda other: flat.at[tiles], planes[part], part)
+            planes[part][p] = flat[tiles]
+        else:
+            to_stack(lambda other: flat.at[tiles], stacks[part], part)
+            stacks[part][q] = flat[tiles]
 
     def second_hop(part):
         plane, pick, stack = planes[part], picks[part], stacks[part]
-        wait_bytes(plane.at[pl.ds(0, PLANE - 1)], hop_recv.at[part])
-        for j in range(STACK):
-            pick[j] = plane[state["places"][j]]
-        for bits in FAR_STACK:
-            pltpu.make_async_remote_copy(
-                src_ref=pick.at[q ^ bits], dst_ref=stack.at[q],
-                send_sem=hop_send.at[3 + part], recv_sem=hop_recv.at[3 + part],
-                device_id=in_stack(bits), device_id_type=MESH,
-            ).start()
-        stack[q] = pick[q]
+        if PARTS[part][2]:
+            wait_bytes(plane.at[pl.ds(0, PLANE - 1)], hop_recv.at[part])
+            for j in range(STACK):
+                pick[j] = plane[state["from_plane"][j]]
+            to_stack(lambda other: pick.at[other], stack, n + part)
+            stack[q] = pick[q]
+        else:
+            wait_bytes(stack.at[pl.ds(0, STACK - 1)], hop_recv.at[part])
+            for j in range(PLANE):
+                pick[j] = stack[state["from_stack"][j]]
+            to_plane(lambda other: pick.at[other], plane, n + part)
+            plane[p] = pick[p]
 
     def finish(part):
-        tiles, stack = pl.ds(*PARTS[part]), stacks[part]
-        wait_bytes(stack.at[pl.ds(0, STACK - 1)], hop_recv.at[3 + part])
-        out[tiles] = stack[state["mine"]].astype(F32)
-
-    def drain():
-        for d in range(4):
+        first, count, plane_first = PARTS[part]
+        if plane_first:
+            wait_bytes(stacks[part].at[pl.ds(0, STACK - 1)], hop_recv.at[n + part])
+            mine = stacks[part][state["mine"][1]].astype(OUT)
+        else:
+            wait_bytes(planes[part].at[pl.ds(0, PLANE - 1)], hop_recv.at[n + part])
+            mine = planes[part][state["mine"][0]].astype(OUT)
+        for i in range(0, count, 2):
+            b = ORDER[(first + i) // 2]
+            out[2 * b:2 * b + 2] = mine[i:i + 2]
+
+    def drain_faces(*ds):
+        for d in ds:
             @pl.when(has[d])
             def _():
                 wait_bytes(own.at[d], send_sem.at[d])
-        for part in range(len(PARTS)):
-            wait_bytes(planes[part].at[pl.ds(0, PLANE - 1)], hop_send.at[part])
-            wait_bytes(stacks[part].at[pl.ds(0, STACK - 1)], hop_send.at[3 + part])
+    def drain_parts(*parts):
+        for part in parts:
+            plane_hop, stack_hop = (part, n + part) if PARTS[part][2] else (n + part, part)
+            wait_bytes(planes[part].at[pl.ds(0, PLANE - 1)], hop_send.at[plane_hop])
+            wait_bytes(stacks[part].at[pl.ds(0, STACK - 1)], hop_send.at[stack_hop])
 
     actions = dict(
-        greet=greet, exchange=exchange, arrived=arrived, gather=gather, band=band_part, put_band=put_band,
+        greet=greet, exchange=exchange, arrived=arrived, gather=gather, gather_if=gather_if, band=band_part, put_band=put_band,
         face_loads=face_loads, face=face_product, block=face_block, owners=owners, first=first_hop, second=second_hop,
-        finish=finish, drain=drain,
+        finish=finish, drain_faces=drain_faces, drain_parts=drain_parts,
     )
     load_panel.wait()
     load_rows.wait()
@@ -245,10 +290,14 @@
         actions[name](*numbers)
 
 
+def store(blocks, out):
+    out[...] = blocks[...].astype(F32)
+
+
 def shards(panel, band, faces, face_rows, owner):
     blocks = pl.pallas_call(
         kernel,
-        out_shape=jax.ShapeDtypeStruct((TILES, 16, 128), F32),
+        out_shape=pltpu.VMEM((TILES, 16, 128), OUT),
         in_specs=[pl.BlockSpec(memory_space=pl.ANY)] * 5,
         out_specs=pl.BlockSpec(memory_space=pltpu.VMEM),
         scratch_shapes=[
@@ -262,18 +311,26 @@
             pltpu.VMEM((4, 2 * K, F), BF16),
             pltpu.VMEM((K, 128), F32),
             pltpu.VMEM((TILES, 16, 128), BF16),
-            *[pltpu.VMEM((PLANE, count, 16, 128), BF16) for _, count in PARTS],
-            *[pltpu.VMEM((STACK, count, 16, 128), BF16) for _, count in PARTS * 2],
+            *[pltpu.VMEM((PLANE, count, 16, 128), BF16) for _, count, _ in PARTS * 2],
+            *[pltpu.VMEM((STACK, count, 16, 128), BF16) for _, count, _ in PARTS],
             pltpu.SemaphoreType.DMA((3 + NB + 4,)),
             pltpu.SemaphoreType.DMA((4,)),
             pltpu.SemaphoreType.DMA((4,)),
-            pltpu.SemaphoreType.DMA((6,)),
-            pltpu.SemaphoreType.DMA((6,)),
+            pltpu.SemaphoreType.DMA((2 * len(PARTS),)),
+            pltpu.SemaphoreType.DMA((2 * len(PARTS),)),
         ],
         compiler_params=pltpu.CompilerParams(collective_id=0, has_side_effects=True, vmem_limit_bytes=58 << 20),
         name="coarse_blocks",
     )(panel[0, 0], band[0, 0], faces[0, 0], face_rows[0, 0], owner.reshape(1, NX * NY))
-    return blocks.reshape(1, 5, 4096)
+    rows = pl.pallas_call(
+        store,
+        out_shape=jax.ShapeDtypeStruct((TILES, 16, 128), F32),
+        in_specs=[pl.BlockSpec(memory_space=pltpu.VMEM)],
+        out_specs=pl.BlockSpec(memory_space=pltpu.VMEM),
+        compiler_params=pltpu.CompilerParams(vmem_limit_bytes=1 << 20),
+        name="store",
+    )(blocks)
+    return rows.reshape(1, 5, 4096)
 
 
 def solution(mesh):

time: 31 us -> 28.9 us (0.932)
  local copies, waits for them, and re-layouts: 1.53 us -> 0 us
  Pallas kernels: 29.3 us -> 28.5 us
    unnamed x1 -> x0, local copies, waits for them, and re-layouts: 1.53 us -> none
    pallas_call x1 -> x2, Pallas kernels: 29.3 us -> 28.5 us  [the longest x1 27.8 us: shards(): pl.pallas_call(kernel, out_shape=pltpu.VMEM((TILES, 16, 128), OUT), in_sp...]
where the time goes in v1:
time: 28.9 us; the launch traced here: 28.5 us
  Pallas kernels  28.5 us (99%)
    pallas_call x1, Pallas kernels, shards(): pl.pallas_call(kernel, out_shape=pltpu.VMEM((TILES, 16, 128), OUT), in_sp...  27.8 us
    pallas_call x1, Pallas kernels, shards(): pl.pallas_call(store, out_shape=jax.ShapeDtypeStruct((TILES, 16, 128), F3...  0.64 us

profile of v1, /device:TPU:1, one launch (start us, length us, event | category | flops | bytes accessed | tf_op | source)
XLA Modules:
  0.0 28.5 jit_solution(4368887417073969217)
XLA Ops:
  0.0 27.8 %coarse_blocks.1.blocks = bf16[10,16,128]{2,1,0:T(8,128)(2,1)S(1)} custom-call(bf16[64,4096]{1,0:T(8,128)(2,1)} %bitcast.8, bf16[8,3,512,512]{3,2,1,0:T(8,128)(2,1)} %bitcast.6, bf16[4,1024,1024]{2,1,0:T(8,128)(2,1)} %bitcast.7, s32[4,1024]{1,0:T(4,128)} %bitcast.9, s32[1,128]{1,0:T(1,128)} %bitcast.10), custom_call_target="tpu_custom_call" | custom-call | tf_op jit(solution)/shard_map/coarse_blocks/pallas_call | solution.py:298
  27.8 0.6 %store.1 = f32[10,16,128]{2,1,0:T(8,128)} custom-call(bf16[10,16,128]{2,1,0:T(8,128)(2,1)S(1)} %coarse_blocks.1.blocks), custom_call_target="tpu_custom_call" | custom-call | tf_op jit(solution)/shard_map/store/pallas_call | solution.py:325

commit v2 on v1

--- a/solution.py
+++ b/solution.py
@@ -14,7 +14,7 @@
 K, R, TB, NB, F = 64, 4096, 512, 8, 1024
 TILES = 10
 ORDER = [0, 3, 4, 1, 2]
-PARTS = [(0, 2, True), (2, 4, True), (6, 4, False)]
+PARTS = [(0, 2, True), (2, 2, True), (4, 2, True), (6, 4, False)]
 STEPS = [
     ('gather', 0),
     ('gather', 1),
@@ -33,25 +33,27 @@
     ('face', 1),
     ('face', 2),
     ('face', 3),
+    ('near_block',),
+    ('first', 1),
     ('owners',),
-    ('arrived', 2),
-    ('block', 2),
-    ('arrived', 3),
-    ('block', 3),
-    ('first', 1),
     ('arrived', 0),
     ('block', 0),
     ('arrived', 1),
     ('block', 1),
+    ('first', 3),
+    ('far_block',),
     ('first', 2),
     ('second', 0),
+    ('second', 1),
+    ('second', 3),
     ('second', 2),
-    ('second', 1),
     ('finish', 0),
     ('finish', 1),
+    ('finish', 3),
     ('finish', 2),
+    ('finish_y',),
     ('drain_faces', 0, 1, 2, 3),
-    ('drain_parts', 0, 1, 2),
+    ('drain_parts', 0, 1, 2, 3),
 ]
 BAND_ORDER = [(1, 4), (2, 4), (3, 8), (4, 8), (5, 8), (6, 8), (7, 8), (0, 8)]
 FAR_PLANE = [(2, 2), (2, 1), (2, 3), (1, 2), (3, 2), (2, 0), (0, 2), (1, 1), (1, 3), (3, 1), (3, 3), (1, 0), (3, 0), (0, 1), (0, 3)]
@@ -195,6 +197,23 @@
         for h in range(2):
             columns = slice(h * 512, (h + 1) * 512)
             pair[d, :, columns] = split(dot_nn(own[d], fv[d, :, columns]))
+
+    same_chip = 3 - (y & 1)
+    other_chip = 5 - same_chip
+    has_other = jnp.logical_and(y > 0, y < NY - 1)
+
+    def near_block():
+        wait_bytes(remote.at[same_chip], recv_sem.at[same_chip])
+        block = dot_nt(pair[same_chip], remote[same_chip])
+        put(3, block[:K] + block[K:])
+
+    def far_block():
+        @pl.when(has_other)
+        def _():
+            wait_bytes(remote.at[other_chip], recv_sem.at[other_chip])
+
+        block = dot_nt(pair[other_chip], remote[other_chip])
+        put(4, jnp.where(has_other, block[:K] + block[K:], 0.0))
 
     def face_block(d):
         block = dot_nt(pair[d], remote[d])
@@ -266,7 +285,16 @@
             mine = planes[part][state["mine"][0]].astype(OUT)
         for i in range(0, count, 2):
             b = ORDER[(first + i) // 2]
-            out[2 * b:2 * b + 2] = mine[i:i + 2]
+            if b in (3, 4):
+                state[b] = mine[i:i + 2]
+            else:
+                out[2 * b:2 * b + 2] = mine[i:i + 2]
+
+    def finish_y():
+        lower_first = (jnp.zeros((2, 16, 128), jnp.int32) + state["mine"][1]) & 1 == 1
+        near, far = state[3].astype(F32), state[4].astype(F32)
+        out[6:8] = jnp.where(lower_first, near, far).astype(OUT)
+        out[8:10] = jnp.where(lower_first, far, near).astype(OUT)
 
     def drain_faces(*ds):
         for d in ds:
@@ -282,7 +310,7 @@
     actions = dict(
         greet=greet, exchange=exchange, arrived=arrived, gather=gather, gather_if=gather_if, band=band_part, put_band=put_band,
         face_loads=face_loads, face=face_product, block=face_block, owners=owners, first=first_hop, second=second_hop,
-        finish=finish, drain_faces=drain_faces, drain_parts=drain_parts,
+        finish=finish, drain_faces=drain_faces, near_block=near_block, far_block=far_block, finish_y=finish_y, drain_parts=drain_parts,
     )
     load_panel.wait()
     load_rows.wait()

time: 28.9 us -> 28.5 us (0.986); the launches traced: 28.5 us -> 28.4 us
  no operation moved by 1% of the time
where the time goes in v2:
time: 28.5 us; the launch traced here: 28.4 us
  Pallas kernels  28.4 us (100%)
    pallas_call x1, Pallas kernels, shards(): pl.pallas_call(kernel, out_shape=pltpu.VMEM((TILES, 16, 128), OUT), in_sp...  27.8 us
    pallas_call x1, Pallas kernels, shards(): pl.pallas_call(store, out_shape=jax.ShapeDtypeStruct((TILES, 16, 128), F3...  0.64 us

profile of v2, /device:TPU:1, one launch (start us, length us, event | category | flops | bytes accessed | tf_op | source)
XLA Modules:
  0.0 28.4 jit_solution(5055793450460951008)
XLA Ops:
  0.0 27.8 %coarse_blocks.1.blocks = bf16[10,16,128]{2,1,0:T(8,128)(2,1)S(1)} custom-call(bf16[64,4096]{1,0:T(8,128)(2,1)} %bitcast.8, bf16[8,3,512,512]{3,2,1,0:T(8,128)(2,1)} %bitcast.6, bf16[4,1024,1024]{2,1,0:T(8,128)(2,1)} %bitcast.7, s32[4,1024]{1,0:T(4,128)} %bitcast.9, s32[1,128]{1,0:T(1,128)} %bitcast.10), custom_call_target="tpu_custom_call" | custom-call | tf_op jit(solution)/shard_map/coarse_blocks/pallas_call | solution.py:326
  27.8 0.6 %store.1 = f32[10,16,128]{2,1,0:T(8,128)} custom-call(bf16[10,16,128]{2,1,0:T(8,128)(2,1)S(1)} %coarse_blocks.1.blocks), custom_call_target="tpu_custom_call" | custom-call | tf_op jit(solution)/shard_map/store/pallas_call | solution.py:353

commit v3 on v2

--- a/solution.py
+++ b/solution.py
@@ -29,16 +29,16 @@
     ('put_band',),
     ('first', 0),
     ('face_loads', 0, 1, 2, 3),
+    ('face_y', 1),
+    ('near_block',),
+    ('first', 1),
+    ('face_y', 0),
     ('face', 0),
     ('face', 1),
-    ('face', 2),
-    ('face', 3),
-    ('near_block',),
-    ('first', 1),
     ('owners',),
     ('arrived', 0),
+    ('arrived', 1),
     ('block', 0),
-    ('arrived', 1),
     ('block', 1),
     ('first', 3),
     ('far_block',),
@@ -121,12 +121,13 @@
         return copy
 
     load_panel, load_rows = load(panel, pv), load(rows, rv)
+
+    for a, b in FAR_PLANE:
+        hello(in_plane(a, b))
+
     load_band = [load(band.at[b], bv.at[b]) for b in range(NB)]
     load_faces = [load(faces.at[d], fv.at[d]) for d in range(4)]
     load_owner = load(owner, ov)
-
-    for a, b in FAR_PLANE:
-        hello(in_plane(a, b))
 
     def greet():
         pl.semaphore_wait(barrier, PLANE + STACK - 2 + sum(far.astype(jnp.int32) for far in beyond))
@@ -166,9 +167,9 @@
                 gather(d)
 
     def put(b, block):
-        tmp[:, :K] = block
-        even = tmp[pl.ds(0, 32, 2), :]
-        odd = tmp[pl.ds(1, 32, 2), :]
+        tmp[b, :, :K] = block
+        even = tmp[b, pl.ds(0, 32, 2), :]
+        odd = tmp[b, pl.ds(1, 32, 2), :]
         slot = 2 * ORDER.index(b)
         flat[slot:slot + 2] = jnp.concatenate([even[:, :K], odd[:, :K]], axis=1).astype(BF16).reshape(2, 16, 128)
 
@@ -201,6 +202,9 @@
     same_chip = 3 - (y & 1)
     other_chip = 5 - same_chip
     has_other = jnp.logical_and(y > 0, y < NY - 1)
+
+    def face_y(same):
+        face_product(same_chip if same else other_chip)
 
     def near_block():
         wait_bytes(remote.at[same_chip], recv_sem.at[same_chip])
@@ -310,7 +314,7 @@
     actions = dict(
         greet=greet, exchange=exchange, arrived=arrived, gather=gather, gather_if=gather_if, band=band_part, put_band=put_band,
         face_loads=face_loads, face=face_product, block=face_block, owners=owners, first=first_hop, second=second_hop,
-        finish=finish, drain_faces=drain_faces, near_block=near_block, far_block=far_block, finish_y=finish_y, drain_parts=drain_parts,
+        finish=finish, drain_faces=drain_faces, near_block=near_block, face_y=face_y, far_block=far_block, finish_y=finish_y, drain_parts=drain_parts,
     )
     load_panel.wait()
     load_rows.wait()
@@ -337,7 +341,7 @@
             pltpu.VMEM((4, K, F), BF16),
             pltpu.VMEM((4, K, F), BF16),
             pltpu.VMEM((4, 2 * K, F), BF16),
-            pltpu.VMEM((K, 128), F32),
+            pltpu.VMEM((5, K, 128), F32),
             pltpu.VMEM((TILES, 16, 128), BF16),
             *[pltpu.VMEM((PLANE, count, 16, 128), BF16) for _, count, _ in PARTS * 2],
             *[pltpu.VMEM((STACK, count, 16, 128), BF16) for _, count, _ in PARTS],

time: 28.5 us -> 28.3 us (level)
  Pallas kernels: 28.4 us -> 28.1 us
where the time goes in v3:
time: 28.3 us; the launch traced here: 28.2 us
  Pallas kernels  28.1 us (99%)
    pallas_call x1, Pallas kernels, shards(): pl.pallas_call(kernel, out_shape=pltpu.VMEM((TILES, 16, 128), OUT), in_sp...  27.5 us
    pallas_call x1, Pallas kernels, shards(): pl.pallas_call(store, out_shape=jax.ShapeDtypeStruct((TILES, 16, 128), F3...  0.64 us

profile of v3, /device:TPU:1, one launch (start us, length us, event | category | flops | bytes accessed | tf_op | source)
XLA Modules:
  0.0 28.2 jit_solution(12200037554116735319)
XLA Ops:
  0.0 27.5 %coarse_blocks.1.blocks = bf16[10,16,128]{2,1,0:T(8,128)(2,1)S(1)} custom-call(bf16[64,4096]{1,0:T(8,128)(2,1)} %bitcast.8, bf16[8,3,512,512]{3,2,1,0:T(8,128)(2,1)} %bitcast.6, bf16[4,1024,1024]{2,1,0:T(8,128)(2,1)} %bitcast.7, s32[4,1024]{1,0:T(4,128)} %bitcast.9, s32[1,128]{1,0:T(1,128)} %bitcast.10), custom_call_target="tpu_custom_call" | custom-call | tf_op jit(solution)/shard_map/coarse_blocks/pallas_call | solution.py:330
  27.5 0.6 %store.1 = f32[10,16,128]{2,1,0:T(8,128)} custom-call(bf16[10,16,128]{2,1,0:T(8,128)(2,1)S(1)} %coarse_blocks.1.blocks), custom_call_target="tpu_custom_call" | custom-call | tf_op jit(solution)/shard_map/store/pallas_call | solution.py:357

commit v4 on v3

--- a/solution.py
+++ b/solution.py
@@ -91,7 +91,7 @@
     p, q = (y >> 2) * 4 + (x >> 1), (x & 1) * 4 + (y & 3)
 
     def in_plane(a, b):
-        return lax.rem((x >> 1) + b, 4) * 2 + (x & 1), lax.rem((y >> 2) + a, 4) * 4 + (y & 3)
+        return (((x >> 1) + b) & 3) * 2 + (x & 1), (((y >> 2) + a) & 3) * 4 + (y & 3)
 
     def in_stack(bits):
         return x ^ (bits >> 2), y ^ (bits & 3)
@@ -243,7 +243,7 @@
     def to_plane(source, target, sems):
         for a, b in FAR_PLANE:
             pltpu.make_async_remote_copy(
-                src_ref=source(lax.rem((y >> 2) + a, 4) * 4 + lax.rem((x >> 1) + b, 4)), dst_ref=target.at[p],
+                src_ref=source((((y >> 2) + a) & 3) * 4 + (((x >> 1) + b) & 3)), dst_ref=target.at[p],
                 send_sem=hop_send.at[sems], recv_sem=hop_recv.at[sems], device_id=in_plane(a, b), device_id_type=MESH,
             ).start()
 

time: 28.3 us -> 28.3 us (level)
  no operation moved by 1% of the time
where the time goes in v4:
time: 28.3 us; the launch traced here: 28.2 us
  Pallas kernels  28.2 us (100%)
    pallas_call x1, Pallas kernels, shards(): pl.pallas_call(kernel, out_shape=pltpu.VMEM((TILES, 16, 128), OUT), in_sp...  27.5 us
    pallas_call x1, Pallas kernels, shards(): pl.pallas_call(store, out_shape=jax.ShapeDtypeStruct((TILES, 16, 128), F3...  0.64 us

profile of v4, /device:TPU:1, one launch (start us, length us, event | category | flops | bytes accessed | tf_op | source)
XLA Modules:
  0.0 28.2 jit_solution(8156709572562549632)
XLA Ops:
  0.0 27.5 %coarse_blocks.1.blocks = bf16[10,16,128]{2,1,0:T(8,128)(2,1)S(1)} custom-call(bf16[64,4096]{1,0:T(8,128)(2,1)} %bitcast.8, bf16[8,3,512,512]{3,2,1,0:T(8,128)(2,1)} %bitcast.6, bf16[4,1024,1024]{2,1,0:T(8,128)(2,1)} %bitcast.7, s32[4,1024]{1,0:T(4,128)} %bitcast.9, s32[1,128]{1,0:T(1,128)} %bitcast.10), custom_call_target="tpu_custom_call" | custom-call | tf_op jit(solution)/shard_map/coarse_blocks/pallas_call | solution.py:330
  27.5 0.6 %store.1 = f32[10,16,128]{2,1,0:T(8,128)} custom-call(bf16[10,16,128]{2,1,0:T(8,128)(2,1)S(1)} %coarse_blocks.1.blocks), custom_call_target="tpu_custom_call" | custom-call | tf_op jit(solution)/shard_map/store/pallas_call | solution.py:357
